TPU v7x, 128 devices: a whole 4x4x4 slice. The times are simulated.
128 devices in a mesh: kpt: 16 (over y, x_lo, core), aux: 8 (over z, x_hi).
Axes of the slice: x: 4 (x_hi: 2, x_lo: 2; x = x_hi * 2 + x_lo), y: 4, z: 4, core: 2. Of those that a mesh axis runs over, the one named last changes fastest.
Arguments:
- amplitudes: bfloat16 [16, 2, 384, 384], P('kpt'), may hold values from -4 to 4
- integrals: bfloat16 [16, 2, 384, 384], P('kpt'), may hold values from -12 to 12
- left_factor: bfloat16 [16, 16, 16, 384, 384], P('kpt', None, 'aux'), may hold values from -0.109375 to 0.109375
- right_factor: bfloat16 [16, 16, 16, 384, 384], P('kpt', None, 'aux'), may hold values from -0.109375 to 0.109375
- pair_energy: float32 [2], replicated, may hold values from -2 to -0.6
- virt_energy: float32 [16, 384], replicated, may hold values from 0.3 to 3
- kconserve: int32 [16, 16, 16], replicated, may hold values from 0 to 15, as said below
Outputs:
- updated_amplitudes: bfloat16 [16, 2, 384, 384], P('kpt')
Inputs may be any that keep to these rules, and one draw needn't show every extreme that they name: `kconserve`: for fixed first two indices the map over the third index is a permutation of the 16 momenta, with table[i, j, table[i, j, a]] = a; the table is an additive momentum law on relabelled momenta.
All inputs are finite; a program needn't handle non-finite values.
Results may differ from a plain program's by a relative error of at most 0.0055.
Values may be sent and summed in bfloat16 or wider, within the bound.
A program may use at most 64 MiB of HBM per device.

v0:
```python
import jax
import jax.numpy as jnp
from jax import lax
from jax.sharding import PartitionSpec as P

ITERS = 2


def from_behind(value, axis, steps):
    count = lax.axis_size(axis)
    pairs = [(source, (source + steps) % count) for source in range(count)]
    return lax.ppermute(value, axis, pairs)


def on_device(
    amplitudes, integrals, left_factor, right_factor, pair_energy, virt_energy, kconserve
):
    local_count = amplitudes.shape[0]
    pair_count = amplitudes.shape[1]
    virtual = amplitudes.shape[3]
    cycle_size = lax.axis_size("kpt")
    position = lax.axis_index("kpt")
    momenta = local_count * cycle_size
    every_k = jnp.arange(momenta, dtype=jnp.int32)
    own_ids = position * local_count + jnp.arange(local_count, dtype=jnp.int32)
    partner = kconserve[0, 0]
    picked = (own_ids[:, None] == every_k[None, :]).astype(jnp.int32)
    partner_ids = jnp.sum(picked * partner[None, :], axis=1)
    onehot_b = (partner_ids[:, None] == every_k[None, :]).astype(jnp.float32)
    energy_b = jnp.dot(onehot_b, virt_energy, precision=lax.Precision.HIGHEST)
    energy_a = lax.dynamic_slice_in_dim(virt_energy, position * local_count, local_count, 0)
    denominator = (
        pair_energy[None, :, None, None] - energy_a[:, None, :, None] - energy_b[:, None, None, :]
    )
    integral_f = integrals.astype(jnp.float32)

    def contribute(amp_block, source):
        offset = source * local_count
        left_panel = lax.dynamic_slice_in_dim(left_factor, offset, local_count, 1)
        right_panel = lax.dynamic_slice_in_dim(right_factor, offset, local_count, 1)
        halfway = jnp.einsum(
            "jpcd,ijlbd->ijlpcb", amp_block, right_panel, preferred_element_type=jnp.float32
        ).astype(jnp.bfloat16)
        return jnp.einsum(
            "ijlac,ijlpcb->ipab", left_panel, halfway, preferred_element_type=jnp.float32
        )

    def ladder(current):
        zero_sum = jnp.zeros((local_count, pair_count, virtual, virtual), jnp.float32)

        def turn(section, carry):
            totals, amp_block = carry
            totals = totals + contribute(amp_block, (position - section) % cycle_size)
            amp_block = from_behind(amp_block, "kpt", 1)
            return (totals, amp_block)

        totals, amp_block = lax.fori_loop(0, cycle_size - 1, turn, (zero_sum, current))
        return totals + contribute(amp_block, (position - (cycle_size - 1)) % cycle_size)

    current = amplitudes
    for repeat in range(ITERS):
        totals = ladder(current)
        summed = lax.psum(totals, "aux")
        current = ((integral_f + summed) / denominator).astype(jnp.bfloat16)
    return current


def solution(mesh):
    placed = (
        P("kpt", None, None, None),
        P("kpt", None, None, None),
        P("kpt", None, "aux", None, None),
        P("kpt", None, "aux", None, None),
        P(),
        P(),
        P(),
    )
    return jax.shard_map(
        on_device, mesh=mesh, in_specs=placed, out_specs=P("kpt", None, None, None), check_vma=False
    )
```

profile of v0, /device:TPU:0, one launch (start us, length us, event | category | flops | bytes accessed | tf_op | source)
XLA Modules:
  0.0 552.6 jit_solution(7127468051716169413)
XLA Ops:
  7.6 173.3 %while.36 = (s32[]{:T(128)}, f32[1,2,384,384]{2,3,1,0:T(8,128)S(1)}, bf16[1,2,384,384]{3,2,1,0:T(8,128)(2,1)S(1)}, s32[]{:T(128)}, bf16[1,16,2,384,384]{4,3,2,1,...) while((s32[]{:T(128)}, ...), condition=%wide.region_1.2_spmd.clone, body=%wide.region_0.0_spmd.clone.sunk | while | flops 907149312 | bytes 7669553 | solution.py:57
  11.0 8.2 %collective-permute-done = bf16[1,2,384,384]{3,2,1,0:T(8,128)(2,1)S(1)} collective-permute-done((bf16[1,2,384,384]{3,2,1,0:T(8,128)(2,1)S(1)}, bf16[1,2,384,384]{3,2,1,0:T(8,128)(2,1)S(1)}, u32[]{:S(2)}, u32[]{:S(2)}) %collective-permute-start) | collective-permute-done | bytes 589856 | tf_op jit(solution)/shard_map/while/body/eval_jaxpr/ppermute | solution.py:12
  19.3 3.2 fusion.67
  22.5 8.2 %collective-permute-done = bf16[1,2,384,384]{3,2,1,0:T(8,128)(2,1)S(1)} collective-permute-done((bf16[1,2,384,384]{3,2,1,0:T(8,128)(2,1)S(1)}, bf16[1,2,384,384]{3,2,1,0:T(8,128)(2,1)S(1)}, u32[]{:S(2)}, u32[]{:S(2)}) %collective-permute-start) | collective-permute-done | bytes 589856 | tf_op jit(solution)/shard_map/while/body/eval_jaxpr/ppermute | solution.py:12
  30.9 3.2 fusion.67
  34.1 8.2 %collective-permute-done = bf16[1,2,384,384]{3,2,1,0:T(8,128)(2,1)S(1)} collective-permute-done((bf16[1,2,384,384]{3,2,1,0:T(8,128)(2,1)S(1)}, bf16[1,2,384,384]{3,2,1,0:T(8,128)(2,1)S(1)}, u32[]{:S(2)}, u32[]{:S(2)}) %collective-permute-start) | collective-permute-done | bytes 589856 | tf_op jit(solution)/shard_map/while/body/eval_jaxpr/ppermute | solution.py:12
  45.6 8.2 %collective-permute-done = bf16[1,2,384,384]{3,2,1,0:T(8,128)(2,1)S(1)} collective-permute-done((bf16[1,2,384,384]{3,2,1,0:T(8,128)(2,1)S(1)}, bf16[1,2,384,384]{3,2,1,0:T(8,128)(2,1)S(1)}, u32[]{:S(2)}, u32[]{:S(2)}) %collective-permute-start) | collective-permute-done | bytes 589856 | tf_op jit(solution)/shard_map/while/body/eval_jaxpr/ppermute | solution.py:12
  54.0 3.2 fusion.67
  57.2 8.2 %collective-permute-done = bf16[1,2,384,384]{3,2,1,0:T(8,128)(2,1)S(1)} collective-permute-done((bf16[1,2,384,384]{3,2,1,0:T(8,128)(2,1)S(1)}, bf16[1,2,384,384]{3,2,1,0:T(8,128)(2,1)S(1)}, u32[]{:S(2)}, u32[]{:S(2)}) %collective-permute-start) | collective-permute-done | bytes 589856 | tf_op jit(solution)/shard_map/while/body/eval_jaxpr/ppermute | solution.py:12
  68.7 8.2 %collective-permute-done = bf16[1,2,384,384]{3,2,1,0:T(8,128)(2,1)S(1)} collective-permute-done((bf16[1,2,384,384]{3,2,1,0:T(8,128)(2,1)S(1)}, bf16[1,2,384,384]{3,2,1,0:T(8,128)(2,1)S(1)}, u32[]{:S(2)}, u32[]{:S(2)}) %collective-permute-start) | collective-permute-done | bytes 589856 | tf_op jit(solution)/shard_map/while/body/eval_jaxpr/ppermute | solution.py:12
  80.3 8.2 %collective-permute-done = bf16[1,2,384,384]{3,2,1,0:T(8,128)(2,1)S(1)} collective-permute-done((bf16[1,2,384,384]{3,2,1,0:T(8,128)(2,1)S(1)}, bf16[1,2,384,384]{3,2,1,0:T(8,128)(2,1)S(1)}, u32[]{:S(2)}, u32[]{:S(2)}) %collective-permute-start) | collective-permute-done | bytes 589856 | tf_op jit(solution)/shard_map/while/body/eval_jaxpr/ppermute | solution.py:12
  91.8 8.2 %collective-permute-done = bf16[1,2,384,384]{3,2,1,0:T(8,128)(2,1)S(1)} collective-permute-done((bf16[1,2,384,384]{3,2,1,0:T(8,128)(2,1)S(1)}, bf16[1,2,384,384]{3,2,1,0:T(8,128)(2,1)S(1)}, u32[]{:S(2)}, u32[]{:S(2)}) %collective-permute-start) | collective-permute-done | bytes 589856 | tf_op jit(solution)/shard_map/while/body/eval_jaxpr/ppermute | solution.py:12
  103.4 8.2 %collective-permute-done = bf16[1,2,384,384]{3,2,1,0:T(8,128)(2,1)S(1)} collective-permute-done((bf16[1,2,384,384]{3,2,1,0:T(8,128)(2,1)S(1)}, bf16[1,2,384,384]{3,2,1,0:T(8,128)(2,1)S(1)}, u32[]{:S(2)}, u32[]{:S(2)}) %collective-permute-start) | collective-permute-done | bytes 589856 | tf_op jit(solution)/shard_map/while/body/eval_jaxpr/ppermute | solution.py:12
  114.9 8.2 %collective-permute-done = bf16[1,2,384,384]{3,2,1,0:T(8,128)(2,1)S(1)} collective-permute-done((bf16[1,2,384,384]{3,2,1,0:T(8,128)(2,1)S(1)}, bf16[1,2,384,384]{3,2,1,0:T(8,128)(2,1)S(1)}, u32[]{:S(2)}, u32[]{:S(2)}) %collective-permute-start) | collective-permute-done | bytes 589856 | tf_op jit(solution)/shard_map/while/body/eval_jaxpr/ppermute | solution.py:12
  126.5 8.2 %collective-permute-done = bf16[1,2,384,384]{3,2,1,0:T(8,128)(2,1)S(1)} collective-permute-done((bf16[1,2,384,384]{3,2,1,0:T(8,128)(2,1)S(1)}, bf16[1,2,384,384]{3,2,1,0:T(8,128)(2,1)S(1)}, u32[]{:S(2)}, u32[]{:S(2)}) %collective-permute-start) | collective-permute-done | bytes 589856 | tf_op jit(solution)/shard_map/while/body/eval_jaxpr/ppermute | solution.py:12
  134.8 3.2 fusion.67
  138.0 8.2 %collective-permute-done = bf16[1,2,384,384]{3,2,1,0:T(8,128)(2,1)S(1)} collective-permute-done((bf16[1,2,384,384]{3,2,1,0:T(8,128)(2,1)S(1)}, bf16[1,2,384,384]{3,2,1,0:T(8,128)(2,1)S(1)}, u32[]{:S(2)}, u32[]{:S(2)}) %collective-permute-start) | collective-permute-done | bytes 589856 | tf_op jit(solution)/shard_map/while/body/eval_jaxpr/ppermute | solution.py:12
  149.6 8.2 %collective-permute-done = bf16[1,2,384,384]{3,2,1,0:T(8,128)(2,1)S(1)} collective-permute-done((bf16[1,2,384,384]{3,2,1,0:T(8,128)(2,1)S(1)}, bf16[1,2,384,384]{3,2,1,0:T(8,128)(2,1)S(1)}, u32[]{:S(2)}, u32[]{:S(2)}) %collective-permute-start) | collective-permute-done | bytes 589856 | tf_op jit(solution)/shard_map/while/body/eval_jaxpr/ppermute | solution.py:12
  161.1 8.2 %collective-permute-done = bf16[1,2,384,384]{3,2,1,0:T(8,128)(2,1)S(1)} collective-permute-done((bf16[1,2,384,384]{3,2,1,0:T(8,128)(2,1)S(1)}, bf16[1,2,384,384]{3,2,1,0:T(8,128)(2,1)S(1)}, u32[]{:S(2)}, u32[]{:S(2)}) %collective-permute-start) | collective-permute-done | bytes 589856 | tf_op jit(solution)/shard_map/while/body/eval_jaxpr/ppermute | solution.py:12
  169.5 3.2 fusion.67
  172.7 8.2 %collective-permute-done = bf16[1,2,384,384]{3,2,1,0:T(8,128)(2,1)S(1)} collective-permute-done((bf16[1,2,384,384]{3,2,1,0:T(8,128)(2,1)S(1)}, bf16[1,2,384,384]{3,2,1,0:T(8,128)(2,1)S(1)}, u32[]{:S(2)}, u32[]{:S(2)}) %collective-permute-start) | collective-permute-done | bytes 589856 | tf_op jit(solution)/shard_map/while/body/eval_jaxpr/ppermute | solution.py:12
  180.9 3.9 fusion.25
  188.4 88.3 %all-reduce.3.cloned.1.call-done = f32[1,2,384,384]{2,3,1,0:T(8,128)} async-done(((f32[1,2,384,384]{2,3,1,0:T(8,128)}), f32[1,2,384,384]{2,3,1,0:T(8,128)}) %all-reduce.3.cloned.1.call-update) | async-done | bytes 1179664 | tf_op jit(solution)/shard_map/psum | solution.py:63
  278.7 173.3 %while.37 = (s32[]{:T(128)}, f32[1,2,384,384]{2,3,1,0:T(8,128)S(1)}, bf16[1,2,384,384]{3,2,1,0:T(8,128)(2,1)S(1)}, s32[]{:T(128)}, bf16[1,16,2,384,384]{4,3,2,1,...) while((s32[]{:T(128)}, ...), condition=%wide.region_5.6_spmd.clone, body=%wide.region_4.5_spmd.clone.sunk | while | flops 907149312 | bytes 7669553 | solution.py:57
  282.1 8.2 %collective-permute-done.1 = bf16[1,2,384,384]{3,2,1,0:T(8,128)(2,1)S(1)} collective-permute-done((bf16[1,2,384,384]{3,2,1,0:T(8,128)(2,1)S(1)}, bf16[1,2,384,384]{3,2,1,0:T(8,128)(2,1)S(1)}, u32[]{:S(2)}, u32[]{:S(2)}) %collective-permute-start.1) | collective-permute-done | bytes 589856 | tf_op jit(solution)/shard_map/while/body/eval_jaxpr/ppermute | solution.py:12
  293.6 8.2 %collective-permute-done.1 = bf16[1,2,384,384]{3,2,1,0:T(8,128)(2,1)S(1)} collective-permute-done((bf16[1,2,384,384]{3,2,1,0:T(8,128)(2,1)S(1)}, bf16[1,2,384,384]{3,2,1,0:T(8,128)(2,1)S(1)}, u32[]{:S(2)}, u32[]{:S(2)}) %collective-permute-start.1) | collective-permute-done | bytes 589856 | tf_op jit(solution)/shard_map/while/body/eval_jaxpr/ppermute | solution.py:12
  305.2 8.2 %collective-permute-done.1 = bf16[1,2,384,384]{3,2,1,0:T(8,128)(2,1)S(1)} collective-permute-done((bf16[1,2,384,384]{3,2,1,0:T(8,128)(2,1)S(1)}, bf16[1,2,384,384]{3,2,1,0:T(8,128)(2,1)S(1)}, u32[]{:S(2)}, u32[]{:S(2)}) %collective-permute-start.1) | collective-permute-done | bytes 589856 | tf_op jit(solution)/shard_map/while/body/eval_jaxpr/ppermute | solution.py:12
  313.5 3.2 fusion.71
  316.7 8.2 %collective-permute-done.1 = bf16[1,2,384,384]{3,2,1,0:T(8,128)(2,1)S(1)} collective-permute-done((bf16[1,2,384,384]{3,2,1,0:T(8,128)(2,1)S(1)}, bf16[1,2,384,384]{3,2,1,0:T(8,128)(2,1)S(1)}, u32[]{:S(2)}, u32[]{:S(2)}) %collective-permute-start.1) | collective-permute-done | bytes 589856 | tf_op jit(solution)/shard_map/while/body/eval_jaxpr/ppermute | solution.py:12
  328.3 8.2 %collective-permute-done.1 = bf16[1,2,384,384]{3,2,1,0:T(8,128)(2,1)S(1)} collective-permute-done((bf16[1,2,384,384]{3,2,1,0:T(8,128)(2,1)S(1)}, bf16[1,2,384,384]{3,2,1,0:T(8,128)(2,1)S(1)}, u32[]{:S(2)}, u32[]{:S(2)}) %collective-permute-start.1) | collective-permute-done | bytes 589856 | tf_op jit(solution)/shard_map/while/body/eval_jaxpr/ppermute | solution.py:12
  339.8 8.2 %collective-permute-done.1 = bf16[1,2,384,384]{3,2,1,0:T(8,128)(2,1)S(1)} collective-permute-done((bf16[1,2,384,384]{3,2,1,0:T(8,128)(2,1)S(1)}, bf16[1,2,384,384]{3,2,1,0:T(8,128)(2,1)S(1)}, u32[]{:S(2)}, u32[]{:S(2)}) %collective-permute-start.1) | collective-permute-done | bytes 589856 | tf_op jit(solution)/shard_map/while/body/eval_jaxpr/ppermute | solution.py:12
  348.2 3.2 fusion.71
  351.4 8.2 %collective-permute-done.1 = bf16[1,2,384,384]{3,2,1,0:T(8,128)(2,1)S(1)} collective-permute-done((bf16[1,2,384,384]{3,2,1,0:T(8,128)(2,1)S(1)}, bf16[1,2,384,384]{3,2,1,0:T(8,128)(2,1)S(1)}, u32[]{:S(2)}, u32[]{:S(2)}) %collective-permute-start.1) | collective-permute-done | bytes 589856 | tf_op jit(solution)/shard_map/while/body/eval_jaxpr/ppermute | solution.py:12
  359.7 3.2 fusion.71
  362.9 8.2 %collective-permute-done.1 = bf16[1,2,384,384]{3,2,1,0:T(8,128)(2,1)S(1)} collective-permute-done((bf16[1,2,384,384]{3,2,1,0:T(8,128)(2,1)S(1)}, bf16[1,2,384,384]{3,2,1,0:T(8,128)(2,1)S(1)}, u32[]{:S(2)}, u32[]{:S(2)}) %collective-permute-start.1) | collective-permute-done | bytes 589856 | tf_op jit(solution)/shard_map/while/body/eval_jaxpr/ppermute | solution.py:12
  374.5 8.2 %collective-permute-done.1 = bf16[1,2,384,384]{3,2,1,0:T(8,128)(2,1)S(1)} collective-permute-done((bf16[1,2,384,384]{3,2,1,0:T(8,128)(2,1)S(1)}, bf16[1,2,384,384]{3,2,1,0:T(8,128)(2,1)S(1)}, u32[]{:S(2)}, u32[]{:S(2)}) %collective-permute-start.1) | collective-permute-done | bytes 589856 | tf_op jit(solution)/shard_map/while/body/eval_jaxpr/ppermute | solution.py:12
  382.8 3.2 fusion.71
  386.0 8.2 %collective-permute-done.1 = bf16[1,2,384,384]{3,2,1,0:T(8,128)(2,1)S(1)} collective-permute-done((bf16[1,2,384,384]{3,2,1,0:T(8,128)(2,1)S(1)}, bf16[1,2,384,384]{3,2,1,0:T(8,128)(2,1)S(1)}, u32[]{:S(2)}, u32[]{:S(2)}) %collective-permute-start.1) | collective-permute-done | bytes 589856 | tf_op jit(solution)/shard_map/while/body/eval_jaxpr/ppermute | solution.py:12
  394.4 3.2 fusion.71
  397.6 8.2 %collective-permute-done.1 = bf16[1,2,384,384]{3,2,1,0:T(8,128)(2,1)S(1)} collective-permute-done((bf16[1,2,384,384]{3,2,1,0:T(8,128)(2,1)S(1)}, bf16[1,2,384,384]{3,2,1,0:T(8,128)(2,1)S(1)}, u32[]{:S(2)}, u32[]{:S(2)}) %collective-permute-start.1) | collective-permute-done | bytes 589856 | tf_op jit(solution)/shard_map/while/body/eval_jaxpr/ppermute | solution.py:12
  409.1 8.2 %collective-permute-done.1 = bf16[1,2,384,384]{3,2,1,0:T(8,128)(2,1)S(1)} collective-permute-done((bf16[1,2,384,384]{3,2,1,0:T(8,128)(2,1)S(1)}, bf16[1,2,384,384]{3,2,1,0:T(8,128)(2,1)S(1)}, u32[]{:S(2)}, u32[]{:S(2)}) %collective-permute-start.1) | collective-permute-done | bytes 589856 | tf_op jit(solution)/shard_map/while/body/eval_jaxpr/ppermute | solution.py:12
  417.5 3.2 fusion.71
  420.7 8.2 %collective-permute-done.1 = bf16[1,2,384,384]{3,2,1,0:T(8,128)(2,1)S(1)} collective-permute-done((bf16[1,2,384,384]{3,2,1,0:T(8,128)(2,1)S(1)}, bf16[1,2,384,384]{3,2,1,0:T(8,128)(2,1)S(1)}, u32[]{:S(2)}, u32[]{:S(2)}) %collective-permute-start.1) | collective-permute-done | bytes 589856 | tf_op jit(solution)/shard_map/while/body/eval_jaxpr/ppermute | solution.py:12
  432.2 8.2 %collective-permute-done.1 = bf16[1,2,384,384]{3,2,1,0:T(8,128)(2,1)S(1)} collective-permute-done((bf16[1,2,384,384]{3,2,1,0:T(8,128)(2,1)S(1)}, bf16[1,2,384,384]{3,2,1,0:T(8,128)(2,1)S(1)}, u32[]{:S(2)}, u32[]{:S(2)}) %collective-permute-start.1) | collective-permute-done | bytes 589856 | tf_op jit(solution)/shard_map/while/body/eval_jaxpr/ppermute | solution.py:12
  440.6 3.2 fusion.71
  443.8 8.2 %collective-permute-done.1 = bf16[1,2,384,384]{3,2,1,0:T(8,128)(2,1)S(1)} collective-permute-done((bf16[1,2,384,384]{3,2,1,0:T(8,128)(2,1)S(1)}, bf16[1,2,384,384]{3,2,1,0:T(8,128)(2,1)S(1)}, u32[]{:S(2)}, u32[]{:S(2)}) %collective-permute-start.1) | collective-permute-done | bytes 589856 | tf_op jit(solution)/shard_map/while/body/eval_jaxpr/ppermute | solution.py:12
  452.0 3.9 fusion.24
  455.9 87.2 %all-reduce.5.cloned.1.call-done = f32[1,2,384,384]{2,3,1,0:T(8,128)} async-done(((f32[1,2,384,384]{2,3,1,0:T(8,128)}), f32[1,2,384,384]{2,3,1,0:T(8,128)}) %all-reduce.5.cloned.1.call-update) | async-done | bytes 1179664 | tf_op jit(solution)/shard_map/psum | solution.py:63
  (101 shorter events, 70.2 us)
Async XLA Ops:
  6.5 179.7 %copy-start = (f32[16,384]{1,0:T(8,128)S(1)}, f32[16,384]{1,0:T(8,128)}, u32[]{:S(2)}) copy-start(f32[16,384]{1,0:T(8,128)} %param.16) | copy-start | bytes 73732
  6.5 1.1 copy-start.1
  6.5 270.2 %all-reduce.3.cloned.1.call-start = ((), (), s32[]{:S(2)}) async-start(), calls=%async_computation | async-start | bytes 2359296 | tf_op jit(solution)/shard_map/psum | solution.py:63
  7.7 11.5 %collective-permute-start = (bf16[1,2,384,384]{3,2,1,0:T(8,128)(2,1)S(1)}, bf16[1,2,384,384]{3,2,1,0:T(8,128)(2,1)S(1)}, u32[]{:S(2)}, u32[]{:S(2)}) collective-permute-start(bf16[1,2,384,384]{3,2,1,0:T(8,128)(2,1)S(1)} %copy.30), channel_id=1, source_target_pairs={{0,8},{8,16},{16,24},{24,32},{32,40},{40,48},{48,56},{56,64},{64,7... | collective-permute-start | bytes 1769480 | tf_op jit(solution)/shard_map/while/body/eval_jaxpr/ppermute | solution.py:12
  19.2 11.5 %collective-permute-start = (bf16[1,2,384,384]{3,2,1,0:T(8,128)(2,1)S(1)}, bf16[1,2,384,384]{3,2,1,0:T(8,128)(2,1)S(1)}, u32[]{:S(2)}, u32[]{:S(2)}) collective-permute-start(bf16[1,2,384,384]{3,2,1,0:T(8,128)(2,1)S(1)} %copy.30), channel_id=1, source_target_pairs={{0,8},{8,16},{16,24},{24,32},{32,40},{40,48},{48,56},{56,64},{64,7... | collective-permute-start | bytes 1769480 | tf_op jit(solution)/shard_map/while/body/eval_jaxpr/ppermute | solution.py:12
  30.8 11.5 %collective-permute-start = (bf16[1,2,384,384]{3,2,1,0:T(8,128)(2,1)S(1)}, bf16[1,2,384,384]{3,2,1,0:T(8,128)(2,1)S(1)}, u32[]{:S(2)}, u32[]{:S(2)}) collective-permute-start(bf16[1,2,384,384]{3,2,1,0:T(8,128)(2,1)S(1)} %copy.30), channel_id=1, source_target_pairs={{0,8},{8,16},{16,24},{24,32},{32,40},{40,48},{48,56},{56,64},{64,7... | collective-permute-start | bytes 1769480 | tf_op jit(solution)/shard_map/while/body/eval_jaxpr/ppermute | solution.py:12
  42.3 11.5 %collective-permute-start = (bf16[1,2,384,384]{3,2,1,0:T(8,128)(2,1)S(1)}, bf16[1,2,384,384]{3,2,1,0:T(8,128)(2,1)S(1)}, u32[]{:S(2)}, u32[]{:S(2)}) collective-permute-start(bf16[1,2,384,384]{3,2,1,0:T(8,128)(2,1)S(1)} %copy.30), channel_id=1, source_target_pairs={{0,8},{8,16},{16,24},{24,32},{32,40},{40,48},{48,56},{56,64},{64,7... | collective-permute-start | bytes 1769480 | tf_op jit(solution)/shard_map/while/body/eval_jaxpr/ppermute | solution.py:12
  53.9 11.5 %collective-permute-start = (bf16[1,2,384,384]{3,2,1,0:T(8,128)(2,1)S(1)}, bf16[1,2,384,384]{3,2,1,0:T(8,128)(2,1)S(1)}, u32[]{:S(2)}, u32[]{:S(2)}) collective-permute-start(bf16[1,2,384,384]{3,2,1,0:T(8,128)(2,1)S(1)} %copy.30), channel_id=1, source_target_pairs={{0,8},{8,16},{16,24},{24,32},{32,40},{40,48},{48,56},{56,64},{64,7... | collective-permute-start | bytes 1769480 | tf_op jit(solution)/shard_map/while/body/eval_jaxpr/ppermute | solution.py:12
  65.4 11.5 %collective-permute-start = (bf16[1,2,384,384]{3,2,1,0:T(8,128)(2,1)S(1)}, bf16[1,2,384,384]{3,2,1,0:T(8,128)(2,1)S(1)}, u32[]{:S(2)}, u32[]{:S(2)}) collective-permute-start(bf16[1,2,384,384]{3,2,1,0:T(8,128)(2,1)S(1)} %copy.30), channel_id=1, source_target_pairs={{0,8},{8,16},{16,24},{24,32},{32,40},{40,48},{48,56},{56,64},{64,7... | collective-permute-start | bytes 1769480 | tf_op jit(solution)/shard_map/while/body/eval_jaxpr/ppermute | solution.py:12
  77.0 11.5 %collective-permute-start = (bf16[1,2,384,384]{3,2,1,0:T(8,128)(2,1)S(1)}, bf16[1,2,384,384]{3,2,1,0:T(8,128)(2,1)S(1)}, u32[]{:S(2)}, u32[]{:S(2)}) collective-permute-start(bf16[1,2,384,384]{3,2,1,0:T(8,128)(2,1)S(1)} %copy.30), channel_id=1, source_target_pairs={{0,8},{8,16},{16,24},{24,32},{32,40},{40,48},{48,56},{56,64},{64,7... | collective-permute-start | bytes 1769480 | tf_op jit(solution)/shard_map/while/body/eval_jaxpr/ppermute | solution.py:12
  88.5 11.5 %collective-permute-start = (bf16[1,2,384,384]{3,2,1,0:T(8,128)(2,1)S(1)}, bf16[1,2,384,384]{3,2,1,0:T(8,128)(2,1)S(1)}, u32[]{:S(2)}, u32[]{:S(2)}) collective-permute-start(bf16[1,2,384,384]{3,2,1,0:T(8,128)(2,1)S(1)} %copy.30), channel_id=1, source_target_pairs={{0,8},{8,16},{16,24},{24,32},{32,40},{40,48},{48,56},{56,64},{64,7... | collective-permute-start | bytes 1769480 | tf_op jit(solution)/shard_map/while/body/eval_jaxpr/ppermute | solution.py:12
  100.1 11.5 %collective-permute-start = (bf16[1,2,384,384]{3,2,1,0:T(8,128)(2,1)S(1)}, bf16[1,2,384,384]{3,2,1,0:T(8,128)(2,1)S(1)}, u32[]{:S(2)}, u32[]{:S(2)}) collective-permute-start(bf16[1,2,384,384]{3,2,1,0:T(8,128)(2,1)S(1)} %copy.30), channel_id=1, source_target_pairs={{0,8},{8,16},{16,24},{24,32},{32,40},{40,48},{48,56},{56,64},{64,7... | collective-permute-start | bytes 1769480 | tf_op jit(solution)/shard_map/while/body/eval_jaxpr/ppermute | solution.py:12
  111.6 11.5 %collective-permute-start = (bf16[1,2,384,384]{3,2,1,0:T(8,128)(2,1)S(1)}, bf16[1,2,384,384]{3,2,1,0:T(8,128)(2,1)S(1)}, u32[]{:S(2)}, u32[]{:S(2)}) collective-permute-start(bf16[1,2,384,384]{3,2,1,0:T(8,128)(2,1)S(1)} %copy.30), channel_id=1, source_target_pairs={{0,8},{8,16},{16,24},{24,32},{32,40},{40,48},{48,56},{56,64},{64,7... | collective-permute-start | bytes 1769480 | tf_op jit(solution)/shard_map/while/body/eval_jaxpr/ppermute | solution.py:12
  123.2 11.5 %collective-permute-start = (bf16[1,2,384,384]{3,2,1,0:T(8,128)(2,1)S(1)}, bf16[1,2,384,384]{3,2,1,0:T(8,128)(2,1)S(1)}, u32[]{:S(2)}, u32[]{:S(2)}) collective-permute-start(bf16[1,2,384,384]{3,2,1,0:T(8,128)(2,1)S(1)} %copy.30), channel_id=1, source_target_pairs={{0,8},{8,16},{16,24},{24,32},{32,40},{40,48},{48,56},{56,64},{64,7... | collective-permute-start | bytes 1769480 | tf_op jit(solution)/shard_map/while/body/eval_jaxpr/ppermute | solution.py:12
  134.7 11.5 %collective-permute-start = (bf16[1,2,384,384]{3,2,1,0:T(8,128)(2,1)S(1)}, bf16[1,2,384,384]{3,2,1,0:T(8,128)(2,1)S(1)}, u32[]{:S(2)}, u32[]{:S(2)}) collective-permute-start(bf16[1,2,384,384]{3,2,1,0:T(8,128)(2,1)S(1)} %copy.30), channel_id=1, source_target_pairs={{0,8},{8,16},{16,24},{24,32},{32,40},{40,48},{48,56},{56,64},{64,7... | collective-permute-start | bytes 1769480 | tf_op jit(solution)/shard_map/while/body/eval_jaxpr/ppermute | solution.py:12
  146.3 11.5 %collective-permute-start = (bf16[1,2,384,384]{3,2,1,0:T(8,128)(2,1)S(1)}, bf16[1,2,384,384]{3,2,1,0:T(8,128)(2,1)S(1)}, u32[]{:S(2)}, u32[]{:S(2)}) collective-permute-start(bf16[1,2,384,384]{3,2,1,0:T(8,128)(2,1)S(1)} %copy.30), channel_id=1, source_target_pairs={{0,8},{8,16},{16,24},{24,32},{32,40},{40,48},{48,56},{56,64},{64,7... | collective-permute-start | bytes 1769480 | tf_op jit(solution)/shard_map/while/body/eval_jaxpr/ppermute | solution.py:12
  157.8 11.5 %collective-permute-start = (bf16[1,2,384,384]{3,2,1,0:T(8,128)(2,1)S(1)}, bf16[1,2,384,384]{3,2,1,0:T(8,128)(2,1)S(1)}, u32[]{:S(2)}, u32[]{:S(2)}) collective-permute-start(bf16[1,2,384,384]{3,2,1,0:T(8,128)(2,1)S(1)} %copy.30), channel_id=1, source_target_pairs={{0,8},{8,16},{16,24},{24,32},{32,40},{40,48},{48,56},{56,64},{64,7... | collective-permute-start | bytes 1769480 | tf_op jit(solution)/shard_map/while/body/eval_jaxpr/ppermute | solution.py:12
  169.4 11.5 %collective-permute-start = (bf16[1,2,384,384]{3,2,1,0:T(8,128)(2,1)S(1)}, bf16[1,2,384,384]{3,2,1,0:T(8,128)(2,1)S(1)}, u32[]{:S(2)}, u32[]{:S(2)}) collective-permute-start(bf16[1,2,384,384]{3,2,1,0:T(8,128)(2,1)S(1)} %copy.30), channel_id=1, source_target_pairs={{0,8},{8,16},{16,24},{24,32},{32,40},{40,48},{48,56},{56,64},{64,7... | collective-permute-start | bytes 1769480 | tf_op jit(solution)/shard_map/while/body/eval_jaxpr/ppermute | solution.py:12
  184.8 1.1 copy-start.2
  184.8 3.5 copy-start.3
  184.9 358.3 %all-reduce.5.cloned.1.call-start = ((), (), s32[]{:S(2)}) async-start(), calls=%async_computation.1 | async-start | bytes 2359296 | tf_op jit(solution)/shard_map/psum | solution.py:63
  278.8 11.5 %collective-permute-start.1 = (bf16[1,2,384,384]{3,2,1,0:T(8,128)(2,1)S(1)}, bf16[1,2,384,384]{3,2,1,0:T(8,128)(2,1)S(1)}, u32[]{:S(2)}, u32[]{:S(2)}) collective-permute-start(bf16[1,2,384,384]{3,2,1,0:T(8,128)(2,1)S(1)} %copy.40), channel_id=1, source_target_pairs={{0,8},{8,16},{16,24},{24,32},{32,40},{40,48},{48,56},{56,64},{64,7... | collective-permute-start | bytes 1769480 | tf_op jit(solution)/shard_map/while/body/eval_jaxpr/ppermute | solution.py:12
  290.3 11.5 %collective-permute-start.1 = (bf16[1,2,384,384]{3,2,1,0:T(8,128)(2,1)S(1)}, bf16[1,2,384,384]{3,2,1,0:T(8,128)(2,1)S(1)}, u32[]{:S(2)}, u32[]{:S(2)}) collective-permute-start(bf16[1,2,384,384]{3,2,1,0:T(8,128)(2,1)S(1)} %copy.40), channel_id=1, source_target_pairs={{0,8},{8,16},{16,24},{24,32},{32,40},{40,48},{48,56},{56,64},{64,7... | collective-permute-start | bytes 1769480 | tf_op jit(solution)/shard_map/while/body/eval_jaxpr/ppermute | solution.py:12
  301.9 11.5 %collective-permute-start.1 = (bf16[1,2,384,384]{3,2,1,0:T(8,128)(2,1)S(1)}, bf16[1,2,384,384]{3,2,1,0:T(8,128)(2,1)S(1)}, u32[]{:S(2)}, u32[]{:S(2)}) collective-permute-start(bf16[1,2,384,384]{3,2,1,0:T(8,128)(2,1)S(1)} %copy.40), channel_id=1, source_target_pairs={{0,8},{8,16},{16,24},{24,32},{32,40},{40,48},{48,56},{56,64},{64,7... | collective-permute-start | bytes 1769480 | tf_op jit(solution)/shard_map/while/body/eval_jaxpr/ppermute | solution.py:12
  313.4 11.5 %collective-permute-start.1 = (bf16[1,2,384,384]{3,2,1,0:T(8,128)(2,1)S(1)}, bf16[1,2,384,384]{3,2,1,0:T(8,128)(2,1)S(1)}, u32[]{:S(2)}, u32[]{:S(2)}) collective-permute-start(bf16[1,2,384,384]{3,2,1,0:T(8,128)(2,1)S(1)} %copy.40), channel_id=1, source_target_pairs={{0,8},{8,16},{16,24},{24,32},{32,40},{40,48},{48,56},{56,64},{64,7... | collective-permute-start | bytes 1769480 | tf_op jit(solution)/shard_map/while/body/eval_jaxpr/ppermute | solution.py:12
  325.0 11.5 %collective-permute-start.1 = (bf16[1,2,384,384]{3,2,1,0:T(8,128)(2,1)S(1)}, bf16[1,2,384,384]{3,2,1,0:T(8,128)(2,1)S(1)}, u32[]{:S(2)}, u32[]{:S(2)}) collective-permute-start(bf16[1,2,384,384]{3,2,1,0:T(8,128)(2,1)S(1)} %copy.40), channel_id=1, source_target_pairs={{0,8},{8,16},{16,24},{24,32},{32,40},{40,48},{48,56},{56,64},{64,7... | collective-permute-start | bytes 1769480 | tf_op jit(solution)/shard_map/while/body/eval_jaxpr/ppermute | solution.py:12
  336.5 11.5 %collective-permute-start.1 = (bf16[1,2,384,384]{3,2,1,0:T(8,128)(2,1)S(1)}, bf16[1,2,384,384]{3,2,1,0:T(8,128)(2,1)S(1)}, u32[]{:S(2)}, u32[]{:S(2)}) collective-permute-start(bf16[1,2,384,384]{3,2,1,0:T(8,128)(2,1)S(1)} %copy.40), channel_id=1, source_target_pairs={{0,8},{8,16},{16,24},{24,32},{32,40},{40,48},{48,56},{56,64},{64,7... | collective-permute-start | bytes 1769480 | tf_op jit(solution)/shard_map/while/body/eval_jaxpr/ppermute | solution.py:12
  348.1 11.5 %collective-permute-start.1 = (bf16[1,2,384,384]{3,2,1,0:T(8,128)(2,1)S(1)}, bf16[1,2,384,384]{3,2,1,0:T(8,128)(2,1)S(1)}, u32[]{:S(2)}, u32[]{:S(2)}) collective-permute-start(bf16[1,2,384,384]{3,2,1,0:T(8,128)(2,1)S(1)} %copy.40), channel_id=1, source_target_pairs={{0,8},{8,16},{16,24},{24,32},{32,40},{40,48},{48,56},{56,64},{64,7... | collective-permute-start | bytes 1769480 | tf_op jit(solution)/shard_map/while/body/eval_jaxpr/ppermute | solution.py:12
  359.6 11.5 %collective-permute-start.1 = (bf16[1,2,384,384]{3,2,1,0:T(8,128)(2,1)S(1)}, bf16[1,2,384,384]{3,2,1,0:T(8,128)(2,1)S(1)}, u32[]{:S(2)}, u32[]{:S(2)}) collective-permute-start(bf16[1,2,384,384]{3,2,1,0:T(8,128)(2,1)S(1)} %copy.40), channel_id=1, source_target_pairs={{0,8},{8,16},{16,24},{24,32},{32,40},{40,48},{48,56},{56,64},{64,7... | collective-permute-start | bytes 1769480 | tf_op jit(solution)/shard_map/while/body/eval_jaxpr/ppermute | solution.py:12
  371.2 11.5 %collective-permute-start.1 = (bf16[1,2,384,384]{3,2,1,0:T(8,128)(2,1)S(1)}, bf16[1,2,384,384]{3,2,1,0:T(8,128)(2,1)S(1)}, u32[]{:S(2)}, u32[]{:S(2)}) collective-permute-start(bf16[1,2,384,384]{3,2,1,0:T(8,128)(2,1)S(1)} %copy.40), channel_id=1, source_target_pairs={{0,8},{8,16},{16,24},{24,32},{32,40},{40,48},{48,56},{56,64},{64,7... | collective-permute-start | bytes 1769480 | tf_op jit(solution)/shard_map/while/body/eval_jaxpr/ppermute | solution.py:12
  382.7 11.5 %collective-permute-start.1 = (bf16[1,2,384,384]{3,2,1,0:T(8,128)(2,1)S(1)}, bf16[1,2,384,384]{3,2,1,0:T(8,128)(2,1)S(1)}, u32[]{:S(2)}, u32[]{:S(2)}) collective-permute-start(bf16[1,2,384,384]{3,2,1,0:T(8,128)(2,1)S(1)} %copy.40), channel_id=1, source_target_pairs={{0,8},{8,16},{16,24},{24,32},{32,40},{40,48},{48,56},{56,64},{64,7... | collective-permute-start | bytes 1769480 | tf_op jit(solution)/shard_map/while/body/eval_jaxpr/ppermute | solution.py:12
  394.3 11.5 %collective-permute-start.1 = (bf16[1,2,384,384]{3,2,1,0:T(8,128)(2,1)S(1)}, bf16[1,2,384,384]{3,2,1,0:T(8,128)(2,1)S(1)}, u32[]{:S(2)}, u32[]{:S(2)}) collective-permute-start(bf16[1,2,384,384]{3,2,1,0:T(8,128)(2,1)S(1)} %copy.40), channel_id=1, source_target_pairs={{0,8},{8,16},{16,24},{24,32},{32,40},{40,48},{48,56},{56,64},{64,7... | collective-permute-start | bytes 1769480 | tf_op jit(solution)/shard_map/while/body/eval_jaxpr/ppermute | solution.py:12
  405.8 11.5 %collective-permute-start.1 = (bf16[1,2,384,384]{3,2,1,0:T(8,128)(2,1)S(1)}, bf16[1,2,384,384]{3,2,1,0:T(8,128)(2,1)S(1)}, u32[]{:S(2)}, u32[]{:S(2)}) collective-permute-start(bf16[1,2,384,384]{3,2,1,0:T(8,128)(2,1)S(1)} %copy.40), channel_id=1, source_target_pairs={{0,8},{8,16},{16,24},{24,32},{32,40},{40,48},{48,56},{56,64},{64,7... | collective-permute-start | bytes 1769480 | tf_op jit(solution)/shard_map/while/body/eval_jaxpr/ppermute | solution.py:12
  417.4 11.5 %collective-permute-start.1 = (bf16[1,2,384,384]{3,2,1,0:T(8,128)(2,1)S(1)}, bf16[1,2,384,384]{3,2,1,0:T(8,128)(2,1)S(1)}, u32[]{:S(2)}, u32[]{:S(2)}) collective-permute-start(bf16[1,2,384,384]{3,2,1,0:T(8,128)(2,1)S(1)} %copy.40), channel_id=1, source_target_pairs={{0,8},{8,16},{16,24},{24,32},{32,40},{40,48},{48,56},{56,64},{64,7... | collective-permute-start | bytes 1769480 | tf_op jit(solution)/shard_map/while/body/eval_jaxpr/ppermute | solution.py:12
  428.9 11.5 %collective-permute-start.1 = (bf16[1,2,384,384]{3,2,1,0:T(8,128)(2,1)S(1)}, bf16[1,2,384,384]{3,2,1,0:T(8,128)(2,1)S(1)}, u32[]{:S(2)}, u32[]{:S(2)}) collective-permute-start(bf16[1,2,384,384]{3,2,1,0:T(8,128)(2,1)S(1)} %copy.40), channel_id=1, source_target_pairs={{0,8},{8,16},{16,24},{24,32},{32,40},{40,48},{48,56},{56,64},{64,7... | collective-permute-start | bytes 1769480 | tf_op jit(solution)/shard_map/while/body/eval_jaxpr/ppermute | solution.py:12
  440.5 11.5 %collective-permute-start.1 = (bf16[1,2,384,384]{3,2,1,0:T(8,128)(2,1)S(1)}, bf16[1,2,384,384]{3,2,1,0:T(8,128)(2,1)S(1)}, u32[]{:S(2)}, u32[]{:S(2)}) collective-permute-start(bf16[1,2,384,384]{3,2,1,0:T(8,128)(2,1)S(1)} %copy.40), channel_id=1, source_target_pairs={{0,8},{8,16},{16,24},{24,32},{32,40},{40,48},{48,56},{56,64},{64,7... | collective-permute-start | bytes 1769480 | tf_op jit(solution)/shard_map/while/body/eval_jaxpr/ppermute | solution.py:12
Sparse Core Ops, SparseCore 0:
  185.0 91.7 all-reduce.2
  456.1 87.0 all-reduce.4
where the time goes:
time: 554 us; the launch traced here: 553 us
  waiting for transfers between devices  422 us (76%)
  matrix products  104 us (19%)
  between operations  13.5 us (2%)
  local copies, waits for them, and re-layouts  5.61 us (1%)
    ppermute x30, waiting for transfers between devices, from_behind(): return lax.ppermute(value, axis, pairs)  246 us
    psum x2, waiting for transfers between devices, on_device(): summed = lax.psum(totals, 'aux')  176 us
    dot_general x32, matrix products, contribute(): jnp.einsum('ijlac,ijlpcb->ipab', left_panel, halfway, preferred_element_t...  103 us
  transfers between devices with their start and end apart: 32, of which 32 were waited for; matrix products, arithmetic and copies ran while one was open for 18% of the time, Pallas kernels for 0%

commit v1 on v0

v1 whole, which is shorter than its diff:
```python
import functools

import jax
import jax.numpy as jnp
from jax import lax
from jax.experimental import pallas as pl
from jax.experimental.pallas import tpu as pltpu
from jax.sharding import PartitionSpec as P

ITERS = 2
MESH = pl.DeviceIdType.MESH
BF16, F32 = jnp.bfloat16, jnp.float32

NV, PAIRS, NK = 384, 2, 16
LOCAL_AUX = 2
CHUNK = NV // 8
PIECE = NV // 4
HALF = NV // 2

AUX = ((1, 0), (3, 0), (2, 0), (0, 1), (1, 1), (3, 1), (2, 1))
ORDER = ((0, 0), (0, 1), (2, 0), (1, 0), (3, 0), (2, 1), (1, 1), (3, 1))

TO_CORE = 0
QUARTER = 8
QUARTER_X = 9
ALONG_Z = 11
OWN_X = 17
OWN_Y = 19
RELAY_X = 27
RELAY_Y = 39
COPIES = 41


def kernel(
    amp_hbm, int_hbm, left_hbm, right_hbm, pair_ref, virt_ref, cons_ref,
    out_hbm,
    cur, left, right, own, half, acc, parts_out, parts_in, ints, den,
    send, recv, rs_send, rs_recv, ag_send, ag_recv, load, edge,
):
    kpt, aux = lax.axis_index("kpt"), lax.axis_index("aux")
    y, xl, core = kpt // 4, (kpt // 2) % 2, kpt % 2
    z, xh = aux // 2, aux % 2

    def device(dy=0, dx=0, dc=0, dz=0, dh=0):
        x = (2 * xh + xl + dx + 2 * dh) % 4
        return (
            (((y + dy) % 4) * 2 + x % 2) * 2 + (core + dc) % 2,
            ((z + dz) % 4) * 2 + x // 2,
        )

    def block(dy, dx):
        return (((y + dy) % 4) * 2 + (xl + dx) % 2) * 2 + core

    partners = [device(dc=1)]
    partners += [device(dy=1), device(dy=3), device(dy=2), device(dx=1), device(dx=3)]
    partners += [device(dz=dz, dh=dh) for dz, dh in AUX]
    barrier = pltpu.get_barrier_semaphore()
    for partner in partners:
        pl.semaphore_signal(barrier, inc=1, device_id=partner, device_id_type=MESH)

    def first_load():
        return pltpu.make_async_copy(amp_hbm.at[0], own.at[0], edge.at[0])

    def ints_load():
        rows = pl.ds(pl.multiple_of(aux * CHUNK, 16), CHUNK)
        return pltpu.make_async_copy(int_hbm.at[0, :, rows], ints, edge.at[1])

    def step_place(step):
        later = (step + 6) // 8
        third = (step + 1) % 3
        dx = (1 - later) * step + later * ((step + 1) // 3 - 1)
        dy = later * (2 - third % 2 + third // 2)
        return ((y + dy) % 4) * 2 + (xl + dx) % 2

    def panel_load(step, which):
        place = step_place(step) * 2
        source, target = ((left_hbm, left), (right_hbm, right))[which]
        return pltpu.make_async_copy(
            source.at[0, pl.ds(place, 2)], target.at[pl.ds(place, 2)], load.at[which, step]
        )

    first_load().start()

    def start_loads(step, unused):
        panel_load(step, 1).start()
        panel_load(step, 0).start()
        return unused

    lax.fori_loop(0, 8, start_loads, 0)
    ints_load().start()

    partner_row = cons_ref[0, 0, kpt]
    energy_b = virt_ref[pl.ds(partner_row, 1), :]
    energy_a = virt_ref[pl.ds(kpt, 1), :]
    row = lax.broadcasted_iota(jnp.int32, (CHUNK, NV), 0) + aux * CHUNK
    lane = lax.broadcasted_iota(jnp.int32, (CHUNK, NV), 1)
    column = jnp.sum(
        jnp.where(row == lane, jnp.broadcast_to(energy_a, (CHUNK, NV)), 0.0), axis=1, keepdims=True
    )
    for p in range(PAIRS):
        den[p] = (pair_ref[p] - column) - energy_b

    ints_load().wait()
    first_load().wait()
    pl.semaphore_wait(barrier, len(partners))

    def copy(it, number, place, start, size, target=None, source=None):
        rows = pl.ds(start if isinstance(start, int) else pl.multiple_of(start, 16), size)
        there = cur.at[it, place, :, rows]
        here = there if source is None else source.at[:, rows]
        return pltpu.make_async_remote_copy(
            src_ref=here, dst_ref=there,
            send_sem=send.at[it, number], recv_sem=recv.at[it, number],
            device_id=device(dc=1) if target is None else target, device_id_type=MESH,
        )

    def to_core(it, which, sibling=False):
        dy, dx = ORDER[which]
        place = block(dy, dx)
        if sibling:
            place = place + 1 - 2 * core
        return copy(it, TO_CORE + which, place, 0, NV)

    def quarter(it, receive=False):
        if receive:
            return copy(it, QUARTER, block(2, 0), z * PIECE, PIECE)
        return copy(it, QUARTER, block(0, 0), z * PIECE, PIECE, device(dy=2), own.at[it])

    def quarter_x(it, way, receive=False):
        start = z * PIECE + way * CHUNK
        target = device(dx=(1, 3)[way])
        return copy(it, QUARTER_X + way, block(2, 1 if receive else 0), start, CHUNK, target)

    def along_z(it, column, way, receive=False):
        dz = (1, 3, 2)[way]
        start = ((z + 4 - dz) % 4 if receive else z) * PIECE
        return copy(it, ALONG_Z + 3 * column + way, block(2, column), start, PIECE, device(dz=dz))

    def own_x(it, way, receive=False):
        if receive:
            return copy(it, OWN_X + way, block(0, 1), way * HALF, HALF)
        target = device(dx=(1, 3)[way])
        return copy(it, OWN_X + way, block(0, 0), way * HALF, HALF, target, own.at[it])

    def own_y(it, piece, way, receive=False):
        number = OWN_Y + 2 * piece + way
        if receive:
            return copy(it, number, block((3, 1)[way], 0), piece * PIECE, PIECE)
        target = device(dy=(1, 3)[way])
        return copy(it, number, block(0, 0), piece * PIECE, PIECE, target, own.at[it])

    def relay_x(it, piece, which, way, receive=False):
        number = RELAY_X + 4 * piece + 2 * which + way
        start = piece * PIECE + way * CHUNK
        target = device(dx=(1, 3)[way])
        return copy(it, number, block((3, 1)[which], 1 if receive else 0), start, CHUNK, target)

    def relay_y(it, way, receive=False):
        target = device(dy=(1, 3)[way])
        dy = (3, 1)[way] if receive else 0
        return copy(it, RELAY_Y + way, block(dy, 1), 3 * PIECE, PIECE, target)

    def aux_index(o, back=False):
        dz, dh = AUX[o]
        return device(dz=4 - dz if back else dz, dh=dh)[1]

    def rs_copy(it, o):
        dz, dh = AUX[o]
        return pltpu.make_async_remote_copy(
            src_ref=parts_out.at[it, o], dst_ref=parts_in.at[it, o],
            send_sem=rs_send.at[it, o], recv_sem=rs_recv.at[it, o],
            device_id=device(dz=dz, dh=dh), device_id_type=MESH,
        )

    def ag_copy(it, o, receive=False):
        dz, dh = AUX[o]
        index = aux_index(o, True) if receive else aux
        rows = pl.ds(pl.multiple_of(index * CHUNK, 16), CHUNK)
        return pltpu.make_async_remote_copy(
            src_ref=own.at[it + 1, :, rows], dst_ref=own.at[it + 1, :, rows],
            send_sem=ag_send.at[it, o], recv_sem=ag_recv.at[it, o],
            device_id=device(dz=dz, dh=dh), device_id_type=MESH,
        )

    def events(it, step):
        if step == 0:
            cur[it, block(0, 0)] = own[it]
            to_core(it, 0).start()
            quarter(it).start()
            for way in range(2):
                own_x(it, way).start()
            for piece in range(4):
                for way in range(2):
                    own_y(it, piece, way).start()
            acc[...] = jnp.zeros_like(acc)

        def take_piece(piece):
            for way in range(2):
                own_y(it, piece, way, True).wait_recv()
            if piece < 3:
                for which in range(2):
                    for way in range(2):
                        relay_x(it, piece, which, way).start()

        if step == 1:
            quarter(it, True).wait_recv()
            for way in range(2):
                quarter_x(it, way).start()
            for way in range(3):
                along_z(it, 0, way).start()
            for way in range(2):
                own_x(it, way, True).wait_recv()
            to_core(it, 1).start()
            for way in range(2):
                relay_y(it, way).start()
            take_piece(0)
        if step == 2:
            for way in range(2):
                quarter_x(it, way, True).wait_recv()
            for way in range(3):
                along_z(it, 1, way).start()
            take_piece(1)
            for way in range(3):
                along_z(it, 0, way, True).wait_recv()
            to_core(it, 2).start()
        if step == 3:
            take_piece(2)
            take_piece(3)
            to_core(it, 3).start()
            to_core(it, 4).start()
        if step == 5:
            for way in range(3):
                along_z(it, 1, way, True).wait_recv()
            to_core(it, 5).start()
        if step == 6:
            for piece in range(3):
                for which in range(2):
                    for way in range(2):
                        relay_x(it, piece, which, way, True).wait_recv()
            for way in range(2):
                relay_y(it, way, True).wait_recv()
            to_core(it, 6).start()
            to_core(it, 7).start()
        to_core(it, step, sibling=True).wait_recv()

    def close(it):
        for o in range(7):
            rows = pl.ds(pl.multiple_of(aux_index(o) * CHUNK, 16), CHUNK)
            for p in range(PAIRS):
                parts_out[it, o, p] = acc[rows, p * NV : (p + 1) * NV].astype(BF16)
            rs_copy(it, o).start()
        for o in range(7):
            rs_copy(it, o).wait_recv()
        rows = pl.ds(pl.multiple_of(aux * CHUNK, 16), CHUNK)
        for p in range(PAIRS):
            total = acc[rows, p * NV : (p + 1) * NV]
            for o in range(7):
                total = total + parts_in[it, o, p].astype(F32)
            own[it + 1, p, rows] = ((ints[p].astype(F32) + total) / den[p]).astype(BF16)
        for o in range(7):
            ag_copy(it, o).start()
        for o in range(7):
            ag_copy(it, o, True).wait_recv()

    def turn(number, unused):
        it, step = number // 8, number % 8
        for at in range(8):
            pl.when(step == at)(functools.partial(events, it, at))

        @pl.when(it == 0)
        def _():
            panel_load(step, 1).wait()
            panel_load(step, 0).wait()

        place = step_place(step) * 2
        for i in range(2):
            amp = cur[it, place + i].reshape(PAIRS * NV, NV)
            panel = right[place + i].reshape(LOCAL_AUX * NV, NV)
            product = lax.dot_general(
                amp, panel, (((1,), (1,)), ((), ())), preferred_element_type=F32
            ).astype(BF16)
            for l in range(LOCAL_AUX):
                for p in range(PAIRS):
                    half[(i * 2 + l) * NV : (i * 2 + l + 1) * NV, p * NV : (p + 1) * NV] = product[
                        p * NV : (p + 1) * NV, l * NV : (l + 1) * NV
                    ]
        panels = jnp.concatenate([left[place + i, l] for i in range(2) for l in range(2)], axis=1)
        acc[...] += jnp.dot(panels, half[...], preferred_element_type=F32)
        pl.when(step == 7)(functools.partial(close, it))
        return unused

    lax.fori_loop(0, 8 * ITERS, turn, 0)

    write = pltpu.make_async_copy(own.at[ITERS], out_hbm.at[0], edge.at[2])
    write.start()

    def drain(it, unused):
        for which in range(8):
            to_core(it, which).wait_send()
        quarter(it).wait_send()
        for way in range(2):
            quarter_x(it, way).wait_send()
            own_x(it, way).wait_send()
            relay_y(it, way).wait_send()
            for piece in range(4):
                own_y(it, piece, way).wait_send()
            for piece in range(3):
                for which in range(2):
                    relay_x(it, piece, which, way).wait_send()
        for column in range(2):
            for way in range(3):
                along_z(it, column, way).wait_send()
        for o in range(7):
            rs_copy(it, o).wait_send()
            ag_copy(it, o).wait_send()
        return unused

    lax.fori_loop(0, ITERS, drain, 0)
    write.wait()


def on_device(*args):
    anywhere = pl.BlockSpec(memory_space=pl.ANY)
    vmem = pl.BlockSpec(memory_space=pltpu.VMEM)
    smem = pl.BlockSpec(memory_space=pltpu.SMEM)
    dma = pltpu.SemaphoreType.DMA
    return pl.pallas_call(
        kernel,
        out_shape=jax.ShapeDtypeStruct((1, PAIRS, NV, NV), BF16),
        in_specs=[anywhere] * 4 + [smem, vmem, smem],
        out_specs=anywhere,
        scratch_shapes=[
            pltpu.VMEM((ITERS, NK, PAIRS, NV, NV), BF16),
            pltpu.VMEM((NK, LOCAL_AUX, NV, NV), BF16),
            pltpu.VMEM((NK, LOCAL_AUX, NV, NV), BF16),
            pltpu.VMEM((ITERS + 1, PAIRS, NV, NV), BF16),
            pltpu.VMEM((2 * LOCAL_AUX * NV, PAIRS * NV), BF16),
            pltpu.VMEM((NV, PAIRS * NV), F32),
            pltpu.VMEM((ITERS, 7, PAIRS, CHUNK, NV), BF16),
            pltpu.VMEM((ITERS, 7, PAIRS, CHUNK, NV), BF16),
            pltpu.VMEM((PAIRS, CHUNK, NV), BF16),
            pltpu.VMEM((PAIRS, CHUNK, NV), F32),
            dma((ITERS, COPIES)),
            dma((ITERS, COPIES)),
            dma((ITERS, 7)),
            dma((ITERS, 7)),
            dma((ITERS, 7)),
            dma((ITERS, 7)),
            dma((2, 8)),
            dma((3,)),
        ],
        compiler_params=pltpu.CompilerParams(
            collective_id=0, has_side_effects=True, vmem_limit_bytes=60 * 2**20
        ),
        cost_estimate=pl.CostEstimate(
            flops=30_000_000_000, bytes_accessed=40_000_000, transcendentals=0
        ),
        name="ladder",
    )(*args)


def solution(mesh):
    placed = (
        P("kpt", None, None, None),
        P("kpt", None, None, None),
        P("kpt", None, "aux", None, None),
        P("kpt", None, "aux", None, None),
        P(),
        P(),
        P(),
    )
    return jax.shard_map(
        on_device, mesh=mesh, in_specs=placed, out_specs=P("kpt", None, None, None), check_vma=False
    )
```

time: 554 us -> 131 us (0.24)
  waiting for transfers between devices: 422 us -> 0 us
  Pallas kernels: 0 us -> 129 us
  matrix products: 104 us -> 0 us
  between operations: 13.5 us -> 0.01 us
    ppermute x30 -> x0, waiting for transfers between devices: 246 us -> none  [from_behind(): return lax.ppermute(value, axis, pairs)]
    psum x2 -> x0, waiting for transfers between devices: 176 us -> none  [on_device(): summed = lax.psum(totals, 'aux')]
    pallas_call x0 -> x1, Pallas kernels: none -> 129 us  [on_device(): pl.pallas_call(kernel, out_shape=jax.ShapeDtypeStruct((1, PAIRS, NV, NV),...]
    dot_general x33 -> x0, matrix products: 104 us -> none  [the longest x32 103 us: contribute(): jnp.einsum('ijlac,ijlpcb->ipab', left_panel, halfway, preferred_element_t...]
  transfers between devices with their start and end apart: 32 -> 0, of which waited for: 32 -> 0; matrix products, arithmetic and copies ran while one was open for 18% -> 0% of each run, Pallas kernels for 0% -> 0%
where the time goes in v1:
time: 131 us
  Pallas kernels  129 us (98%)
  local copies, waits for them, and re-layouts  1.94 us (1%)
    pallas_call x1, Pallas kernels, on_device(): pl.pallas_call(kernel, out_shape=jax.ShapeDtypeStruct((1, PAIRS, NV, NV),...  129 us

profile of v1, /device:TPU:0, one launch (start us, length us, event | category | flops | bytes accessed | tf_op | source)
XLA Modules:
  0.0 130.6 jit_solution(2725717564404914396)
XLA Ops:
  0.0 128.7 %ladder.1 = bf16[1,2,384,384]{3,2,1,0:T(8,128)(2,1)} custom-call(bf16[1,2,384,384]{3,2,1,0:T(8,128)(2,1)} %amp_hbm.1, bf16[1,2,384,384]{3,2,1,0:T(8,128)(2,1)} %int_hbm.1, bf16[1,16,2,384,384]{4,3,2,1,0:T(8,128)(2,1)} %left_hbm.1, bf16[1,16,2,384,384]{4,3,2,1,0:T(8,128)(2,1)} %right_hbm.1, f32[2]{0:T(128)} %pair_ref.1, f32[16,384]{1,0:T(8,128)} %virt_ref.1, ...), custom_call_target="tpu_custom_call" | custom-call | flops 30000001024 | bytes 40000000 | tf_op jit(solution)/shard_map/ladder/pallas_call | solution.py:327
  128.7 1.9 %copy.9 = bf16[1,2,384,384]{3,2,1,0:T(8,128)(2,1)} copy(bf16[1,2,384,384]{3,2,1,0:T(8,128)(2,1)} %ladder.1) | data formatting | bytes 1179648

commit v2 on v0

v2 whole, which is shorter than its diff:
```python
import functools

import jax
import jax.numpy as jnp
from jax import lax
from jax.experimental import pallas as pl
from jax.experimental.pallas import tpu as pltpu
from jax.sharding import PartitionSpec as P

ITERS = 2
MESH = pl.DeviceIdType.MESH
BF16, F32 = jnp.bfloat16, jnp.float32

NV, PAIRS, NK = 384, 2, 16
LOCAL_AUX = 2
CHUNK = NV // 8
PIECE = NV // 4
HALF = NV // 2

AUX = ((0, 1), (2, 1), (1, 1), (3, 1), (2, 0), (1, 0), (3, 0))
ORDER = ((0, 0), (0, 1), (2, 0), (1, 0), (3, 0), (1, 1), (3, 1), (2, 1))

GROUPS = ITERS * PAIRS

TO_CORE = 0
QUARTER, QUARTER_X, OWN_X, RELAYS, SUMS, ROWS = 8, 9, 10, 11, 12, 13
ALONG_Z = 15
OWN_Y = 17
ARRIVALS = 21


SCHEDULE = {
    0: (("panels", 0), ("clear", 0),),
    1: (("clear", 1),),
    2: (("panels", 1), ("quarter", 0), ("own_x", 0), ("piece0", 0),),
    3: (
        ("panels", 2),
        ("piece1", 0),
        ("quarter_x", 0),
        ("z0", 0),
        ("piece2", 0),
        ("piece3", 0),
        ("begin", 1),
    ),
    4: (("panels", 3),),
    5: (("panels", 4), ("relays", 0),),
    6: (("panels", 5), ("quarter", 1),),
    7: (("panels", 6), ("z1", 0), ("own_x", 1), ("piece0", 1),),
    8: (("panels", 7), ("quarter_x", 1), ("piece1", 1),),
    9: (("scatter", 0), ("piece2", 1),),
    10: (("z0", 1), ("piece3", 1), ("denominators", 0),),
    12: (("relays", 1),),
    13: (("update", 0),),
    14: (("z1", 1),),
    16: (("scatter", 1), ("rows_first", 0), ("rows_rest", 0), ("clear", 2),),
    17: (("quarter", 2), ("piece0", 2), ("update", 1), ("piece1", 2), ("own_x", 2),),
    18: (("quarter_x", 2), ("z0", 2), ("piece2", 2), ("piece3", 2),),
    19: (("rows_first", 1),),
    20: (("rows_rest", 1), ("relays", 2),),
    22: (("z1", 2), ("quarter", 3), ("piece0", 3),),
    23: (("own_x", 3), ("piece1", 3),),
    24: (("scatter", 2), ("clear", 3), ("quarter_x", 3), ("piece2", 3),),
    25: (("z0", 3), ("piece3", 3),),
    28: (("relays", 3),),
    29: (("update", 2),),
    30: (("z1", 3),),
}


def kernel(
    amp_hbm, int_hbm, left_hbm, right_hbm, pair_ref, virt_hbm, cons_hbm,
    out_hbm,
    cur, left, right, own, half, acc, parts_out, parts_in, ints, den, virt, cons,
    sent, recv, load, edge,
):
    kpt, aux = lax.axis_index("kpt"), lax.axis_index("aux")
    y, xl, core = kpt // 4, (kpt // 2) % 2, kpt % 2
    z, xh = aux // 2, aux % 2

    def device(dy=0, dx=0, dc=0, dz=0, dh=0):
        x = (2 * xh + xl + dx + 2 * dh) % 4
        return (
            (((y + dy) % 4) * 2 + x % 2) * 2 + (core + dc) % 2,
            ((z + dz) % 4) * 2 + x // 2,
        )

    def block(dy, dx):
        return (((y + dy) % 4) * 2 + (xl + dx) % 2) * 2 + core

    def rows_of(start, size):
        return pl.ds(start if isinstance(start, int) else pl.multiple_of(start, 16), size)

    partners = [device(dc=1)]
    partners += [device(dy=1), device(dy=3), device(dy=2), device(dx=1), device(dx=3)]
    partners += [device(dz=dz, dh=dh) for dz, dh in AUX]
    barrier = pltpu.get_barrier_semaphore()
    for partner in partners:
        pl.semaphore_signal(barrier, inc=1, device_id=partner, device_id_type=MESH)

    def first_load():
        return pltpu.make_async_copy(amp_hbm.at[0], own.at[0], edge.at[0])

    def ints_load():
        return pltpu.make_async_copy(int_hbm.at[0, :, rows_of(aux * CHUNK, CHUNK)], ints, edge.at[1])

    def step_place(step):
        later = (step + 6) // 8
        dx = (1 - later) * step + later * ((step + 1) // 3 - 1)
        third = (step + 1 + dx) % 3
        dy = later * (2 - third % 2 + third // 2)
        return ((y + dy) % 4) * 2 + (xl + dx) % 2

    def panel_loads(step):
        place = step_place(step) * 2
        return [
            pltpu.make_async_copy(
                source.at[0, pl.ds(place, 2)], target.at[pl.ds(place, 2)], load.at[step, which]
            )
            for which, (source, target) in enumerate(((right_hbm, right), (left_hbm, left)))
        ]

    def small_loads():
        return [
            ints_load(),
            pltpu.make_async_copy(virt_hbm, virt, edge.at[2]),
            pltpu.make_async_copy(cons_hbm.at[0, pl.ds(0, 8)], cons, edge.at[3]),
        ]

    first_load().start()
    for one in small_loads():
        one.start()

    def start_loads(step, unused):
        for one in panel_loads(step):
            one.start()
        return unused

    lax.fori_loop(0, 8, start_loads, 0)

    def denominators():
        for one in small_loads():
            one.wait()
        partner_row = cons[0, kpt]
        energy_b = virt[pl.ds(partner_row, 1), :]
        energy_a = virt[pl.ds(kpt, 1), :]
        row = lax.broadcasted_iota(jnp.int32, (CHUNK, NV), 0) + aux * CHUNK
        lane = lax.broadcasted_iota(jnp.int32, (CHUNK, NV), 1)
        column = jnp.sum(
            jnp.where(row == lane, jnp.broadcast_to(energy_a, (CHUNK, NV)), 0.0),
            axis=1, keepdims=True,
        )
        for p in range(PAIRS):
            den[p] = (pair_ref[p] - column) - energy_b

    first_load().wait()
    pl.semaphore_wait(barrier, len(partners))

    def copy(group, number, place, start, size, target=None, first=False):
        it, p = group // PAIRS, group % PAIRS
        there = cur.at[it, place, p, rows_of(start, size)]
        here = own.at[it, p, rows_of(start, size)] if first else there
        return pltpu.make_async_remote_copy(
            src_ref=here, dst_ref=there,
            send_sem=sent.at[0], recv_sem=recv.at[group, number],
            device_id=device(dc=1) if target is None else target, device_id_type=MESH,
        )

    def arrived(group, number, rows):
        it, p = group // PAIRS, group % PAIRS
        if rows > NV:
            there = cur.at[it, pl.ds(0, rows // NV), p]
        else:
            there = cur.at[it, 0, p, pl.ds(0, rows)]
        pltpu.make_async_copy(there, there, recv.at[group, number]).wait()

    def to_core(group, which):
        return copy(group, TO_CORE + which, block(*ORDER[which]), 0, NV, first=which == 0)

    def quarter(group):
        return copy(group, QUARTER, block(0, 0), z * PIECE, PIECE, device(dy=2), True)

    def quarter_x(group, way):
        start = z * PIECE + way * CHUNK
        return copy(group, QUARTER_X, block(2, 0), start, CHUNK, device(dx=(1, 3)[way]))

    def along_z(group, column, way):
        target = device(dz=(1, 3, 2)[way])
        return copy(group, ALONG_Z + column, block(2, column), z * PIECE, PIECE, target)

    def own_x(group, way):
        return copy(group, OWN_X, block(0, 0), way * HALF, HALF, device(dx=(1, 3)[way]), True)

    def own_y(group, piece, way):
        start = ((z + piece) % 4) * PIECE
        return copy(group, OWN_Y + piece, block(0, 0), start, PIECE, device(dy=(1, 3)[way]), True)

    def relay_x(group, piece, which, way):
        start = ((z + piece) % 4) * PIECE + way * CHUNK
        target = device(dx=(1, 3)[way])
        return copy(group, RELAYS, block((3, 1)[which], 0), start, CHUNK, target)

    def relay_y(group, piece, way):
        start = ((z + piece) % 4) * PIECE
        return copy(group, RELAYS, block(0, 1), start, PIECE, device(dy=(1, 3)[way]))

    def aux_index(o):
        dz, dh = AUX[o]
        return device(dz=dz, dh=dh)[1]

    def rs_copy(group, o):
        dz, dh = AUX[o]
        return pltpu.make_async_remote_copy(
            src_ref=parts_out.at[group, o], dst_ref=parts_in.at[group, o],
            send_sem=sent.at[1], recv_sem=recv.at[group, SUMS],
            device_id=device(dz=dz, dh=dh), device_id_type=MESH,
        )

    def ag_copy(group, o):
        it, p = group // PAIRS, group % PAIRS
        dz, dh = AUX[o]
        rows = rows_of(aux * CHUNK, CHUNK)
        return pltpu.make_async_remote_copy(
            src_ref=own.at[it + 1, p, rows], dst_ref=own.at[it + 1, p, rows],
            send_sem=sent.at[1], recv_sem=recv.at[group, ROWS + min(o, 1)],
            device_id=device(dz=dz, dh=dh), device_id_type=MESH,
        )

    def begin_quarter(group):
        quarter(group).start()
        for way in range(2):
            own_y(group, 0, way).start()

    def begin_rest(group):
        for way in range(2):
            own_x(group, way).start()
        for piece in range(1, 4):
            for way in range(2):
                own_y(group, piece, way).start()

    def share_own(group):
        to_core(group, 0).start()
        it, p = group // PAIRS, group % PAIRS
        cur[it, block(0, 0), p] = own[it, p]

    def take_quarter(group):
        arrived(group, QUARTER, PIECE)
        for way in range(3):
            along_z(group, 0, way).start()
        for way in range(2):
            quarter_x(group, way).start()

    def take_own_x(group):
        arrived(group, OWN_X, NV)
        to_core(group, 1).start()
        for piece in range(2, 4):
            for way in range(2):
                relay_y(group, piece, way).start()

    def take_piece(group, piece):
        arrived(group, OWN_Y + piece, 2 * PIECE)
        if piece < 2:
            for which in range(2):
                for way in range(2):
                    relay_x(group, piece, which, way).start()
        elif piece == 3:
            to_core(group, 3).start()
            to_core(group, 4).start()

    def take_quarter_x(group):
        arrived(group, QUARTER_X, PIECE)
        for way in range(3):
            along_z(group, 1, way).start()

    def take_z(group, column):
        arrived(group, ALONG_Z + column, 3 * PIECE)
        to_core(group, (2, 7)[column]).start()

    def take_relays(group):
        arrived(group, RELAYS, 2 * NV)
        to_core(group, 5).start()
        to_core(group, 6).start()

    def scatter(group):
        p = group % PAIRS
        for o in (1, 2, 3, 4, 0, 5, 6):
            rows = rows_of(aux_index(o) * CHUNK, CHUNK)
            parts_out[group, o] = acc[p, rows].astype(BF16)
            rs_copy(group, o).start()

    def update(group):
        it, p = group // PAIRS, group % PAIRS
        arrived(group, SUMS, 7 * CHUNK)
        rows = rows_of(aux * CHUNK, CHUNK)
        total = acc[p, rows]
        for o in range(7):
            total = total + parts_in[group, o].astype(F32)
        own[it + 1, p, rows] = ((ints[p].astype(F32) + total) / den[p]).astype(BF16)
        for o in range(7):
            ag_copy(group, o).start()

    def take_rows_first(group):
        arrived(group, ROWS, CHUNK)
        if group < GROUPS - PAIRS:
            begin_quarter(group + PAIRS)

    def take_rows_rest(group):
        arrived(group, ROWS + 1, 6 * CHUNK)
        if group < GROUPS - PAIRS:
            share_own(group + PAIRS)
            begin_rest(group + PAIRS)

    def begin(group):
        begin_quarter(group)
        begin_rest(group)

    def clear(group):
        acc[group % PAIRS] = jnp.zeros((NV, NV), F32)

    def take_panels(step):
        for one in panel_loads(step):
            one.wait()

    events = {
        "begin": begin, "quarter": take_quarter, "own_x": take_own_x, "quarter_x": take_quarter_x,
        "relays": take_relays, "update": update, "rows_first": take_rows_first,
        "rows_rest": take_rows_rest, "scatter": scatter, "clear": clear, "panels": take_panels,
        "denominators": lambda group: denominators(),
        "piece0": functools.partial(take_piece, piece=0),
        "piece1": functools.partial(take_piece, piece=1),
        "piece2": functools.partial(take_piece, piece=2),
        "piece3": functools.partial(take_piece, piece=3),
        "z0": functools.partial(take_z, column=0),
        "z1": functools.partial(take_z, column=1),
    }

    def turn(number, unused):
        second = (number + 63) // 64 - (number + 62) // 64
        shifted = (number + 62) // 64 - (number + 55) // 64
        place = number + 7 * second - shifted
        group, step = place // 8, place % 8
        it, p = group // PAIRS, group % PAIRS

        def happen(low, high):
            ticks = [at for at in SCHEDULE if low <= at < high]
            if not ticks:
                return
            if high - low == 1:
                for name, which in SCHEDULE[low]:
                    events[name](which)
                return
            middle = (low + high) // 2
            pl.when(number < middle)(lambda: happen(low, middle))
            pl.when(number >= middle)(lambda: happen(middle, high))

        happen(0, 8 * GROUPS)

        def first_product(i):
            place = step_place(step) * 2 + (core if i == 0 else 1 - core)
            panel = right[place].reshape(LOCAL_AUX * NV, NV)
            product = lax.dot_general(
                cur[it, place, p], panel, (((1,), (1,)), ((), ())), preferred_element_type=F32
            ).astype(BF16)
            for l in range(LOCAL_AUX):
                half[(i * 2 + l) * NV : (i * 2 + l + 1) * NV] = product[:, l * NV : (l + 1) * NV]
            return place

        there = cur.at[it, 0, p]
        pltpu.make_async_copy(there, there, recv.at[group, TO_CORE + step]).wait()
        mine, other = first_product(0), first_product(1)
        panels = jnp.concatenate([left[k, l] for k in (mine, other) for l in range(2)], axis=1)
        acc[p] += jnp.dot(panels, half[...], preferred_element_type=F32)
        return unused

    share_own(0)
    begin(0)
    share_own(1)
    lax.fori_loop(0, 8 * GROUPS, turn, 0)
    scatter(GROUPS - 1)
    take_rows_first(GROUPS - 2)
    take_rows_rest(GROUPS - 2)
    writes = [
        pltpu.make_async_copy(own.at[ITERS, p], out_hbm.at[0, p], edge.at[4 + p])
        for p in range(PAIRS)
    ]
    writes[0].start()
    update(GROUPS - 1)
    take_rows_first(GROUPS - 1)
    take_rows_rest(GROUPS - 1)
    writes[1].start()

    there = cur.at[:, pl.ds(0, 15)]
    pltpu.make_async_copy(there, there, sent.at[0]).wait()
    for back in (parts_out, parts_in):
        pltpu.make_async_copy(back, back, sent.at[1]).wait()
    for one in writes:
        one.wait()


def on_device(*args):
    anywhere = pl.BlockSpec(memory_space=pl.ANY)
    smem = pl.BlockSpec(memory_space=pltpu.SMEM)
    dma = pltpu.SemaphoreType.DMA
    return pl.pallas_call(
        kernel,
        out_shape=jax.ShapeDtypeStruct((1, PAIRS, NV, NV), BF16),
        in_specs=[anywhere] * 4 + [smem, anywhere, anywhere],
        out_specs=anywhere,
        scratch_shapes=[
            pltpu.VMEM((ITERS, NK, PAIRS, NV, NV), BF16),
            pltpu.VMEM((NK, LOCAL_AUX, NV, NV), BF16),
            pltpu.VMEM((NK, LOCAL_AUX, NV, NV), BF16),
            pltpu.VMEM((ITERS + 1, PAIRS, NV, NV), BF16),
            pltpu.VMEM((2 * LOCAL_AUX * NV, NV), BF16),
            pltpu.VMEM((PAIRS, NV, NV), F32),
            pltpu.VMEM((GROUPS, 7, CHUNK, NV), BF16),
            pltpu.VMEM((GROUPS, 7, CHUNK, NV), BF16),
            pltpu.VMEM((PAIRS, CHUNK, NV), BF16),
            pltpu.VMEM((PAIRS, CHUNK, NV), F32),
            pltpu.VMEM((NK, NV), F32),
            pltpu.SMEM((8, NK), jnp.int32),
            dma((2,)),
            dma((GROUPS, ARRIVALS)),
            dma((8, 2)),
            dma((6,)),
        ],
        compiler_params=pltpu.CompilerParams(
            collective_id=0, has_side_effects=True, vmem_limit_bytes=60 * 2**20
        ),
        cost_estimate=pl.CostEstimate(
            flops=30_000_000_000, bytes_accessed=40_000_000, transcendentals=0
        ),
        name="ladder",
    )(*args)


def solution(mesh):
    placed = (
        P("kpt", None, None, None),
        P("kpt", None, None, None),
        P("kpt", None, "aux", None, None),
        P("kpt", None, "aux", None, None),
        P(),
        P(),
        P(),
    )
    return jax.shard_map(
        on_device, mesh=mesh, in_specs=placed, out_specs=P("kpt", None, None, None), check_vma=False
    )
```

time: 554 us -> 94.2 us (0.17)
  waiting for transfers between devices: 422 us -> 0 us
  matrix products: 104 us -> 0 us
  Pallas kernels: 0 us -> 92.1 us
  between operations: 13.5 us -> 0.01 us
    ppermute x30 -> x0, waiting for transfers between devices: 246 us -> none  [from_behind(): return lax.ppermute(value, axis, pairs)]
    psum x2 -> x0, waiting for transfers between devices: 176 us -> none  [on_device(): summed = lax.psum(totals, 'aux')]
    dot_general x33 -> x0, matrix products: 104 us -> none  [the longest x32 103 us: contribute(): jnp.einsum('ijlac,ijlpcb->ipab', left_panel, halfway, preferred_element_t...]
    pallas_call x0 -> x1, Pallas kernels: none -> 92.1 us  [on_device(): pl.pallas_call(kernel, out_shape=jax.ShapeDtypeStruct((1, PAIRS, NV, NV),...]
  transfers between devices with their start and end apart: 32 -> 0, of which waited for: 32 -> 0; matrix products, arithmetic and copies ran while one was open for 18% -> 0% of each run, Pallas kernels for 0% -> 0%
where the time goes in v2:
time: 94.2 us; the launch traced here: 94 us
  Pallas kernels  92.1 us (98%)
  local copies, waits for them, and re-layouts  1.94 us (2%)
    pallas_call x1, Pallas kernels, on_device(): pl.pallas_call(kernel, out_shape=jax.ShapeDtypeStruct((1, PAIRS, NV, NV),...  92.1 us
    unnamed x1, local copies, waits for them, and re-layouts  1.94 us

profile of v2, /device:TPU:0, one launch (start us, length us, event | category | flops | bytes accessed | tf_op | source)
XLA Modules:
  0.0 94.0 jit_solution(10138661573022055886)
XLA Ops:
  0.0 92.1 %ladder.1 = bf16[1,2,384,384]{3,2,1,0:T(8,128)(2,1)} custom-call(bf16[1,2,384,384]{3,2,1,0:T(8,128)(2,1)} %amp_hbm.1, bf16[1,2,384,384]{3,2,1,0:T(8,128)(2,1)} %int_hbm.1, bf16[1,16,2,384,384]{4,3,2,1,0:T(8,128)(2,1)} %left_hbm.1, bf16[1,16,2,384,384]{4,3,2,1,0:T(8,128)(2,1)} %right_hbm.1, f32[2]{0:T(128)} %pair_ref.1, f32[16,384]{1,0:T(8,128)} %virt_hbm.1, ...), custom_call_target="tpu_custom_call" | custom-call | flops 30000001024 | bytes 40000000 | tf_op jit(solution)/shard_map/ladder/pallas_call | solution.py:403
  92.1 1.9 %copy.9 = bf16[1,2,384,384]{3,2,1,0:T(8,128)(2,1)} copy(bf16[1,2,384,384]{3,2,1,0:T(8,128)(2,1)} %ladder.1) | data formatting | bytes 1179648

commit v3 on v2

--- a/solution.py
+++ b/solution.py
@@ -47,8 +47,8 @@
     6: (("panels", 5), ("quarter", 1),),
     7: (("panels", 6), ("z1", 0), ("own_x", 1), ("piece0", 1),),
     8: (("panels", 7), ("quarter_x", 1), ("piece1", 1),),
-    9: (("scatter", 0), ("piece2", 1),),
-    10: (("z0", 1), ("piece3", 1), ("denominators", 0),),
+    9: (("scatter", 0), ("piece2", 1), ("z0", 1),),
+    10: (("piece3", 1), ("denominators", 0),),
     12: (("relays", 1),),
     13: (("update", 0),),
     14: (("z1", 1),),
@@ -68,9 +68,9 @@
 
 
 def kernel(
-    amp_hbm, int_hbm, left_hbm, right_hbm, pair_ref, virt_hbm, cons_hbm,
-    out_hbm,
-    cur, left, right, own, half, acc, parts_out, parts_in, ints, den, virt, cons,
+    amp_hbm, int_hbm, left_hbm, right_hbm, pair_hbm, virt_hbm, cons_hbm,
+    out_ref,
+    cur, left, right, own, half, acc, parts_out, parts_in, ints, den, virt, cons, pair,
     sent, recv, load, edge,
 ):
     kpt, aux = lax.axis_index("kpt"), lax.axis_index("aux")
@@ -97,8 +97,8 @@
     for partner in partners:
         pl.semaphore_signal(barrier, inc=1, device_id=partner, device_id_type=MESH)
 
-    def first_load():
-        return pltpu.make_async_copy(amp_hbm.at[0], own.at[0], edge.at[0])
+    def first_load(p):
+        return pltpu.make_async_copy(amp_hbm.at[0, p], own.at[0, p], edge.at[4 + p])
 
     def ints_load():
         return pltpu.make_async_copy(int_hbm.at[0, :, rows_of(aux * CHUNK, CHUNK)], ints, edge.at[1])
@@ -124,9 +124,11 @@
             ints_load(),
             pltpu.make_async_copy(virt_hbm, virt, edge.at[2]),
             pltpu.make_async_copy(cons_hbm.at[0, pl.ds(0, 8)], cons, edge.at[3]),
+            pltpu.make_async_copy(pair_hbm, pair, edge.at[6]),
         ]
 
-    first_load().start()
+    first_load(0).start()
+    first_load(1).start()
     for one in small_loads():
         one.start()
 
@@ -150,9 +152,9 @@
             axis=1, keepdims=True,
         )
         for p in range(PAIRS):
-            den[p] = (pair_ref[p] - column) - energy_b
-
-    first_load().wait()
+            den[p] = (pair[p] - column) - energy_b
+
+    first_load(0).wait()
     pl.semaphore_wait(barrier, len(partners))
 
     def copy(group, number, place, start, size, target=None, first=False):
@@ -219,8 +221,9 @@
         it, p = group // PAIRS, group % PAIRS
         dz, dh = AUX[o]
         rows = rows_of(aux * CHUNK, CHUNK)
+        there = out_ref.at[0, p, rows] if it == ITERS - 1 else own.at[it + 1, p, rows]
         return pltpu.make_async_remote_copy(
-            src_ref=own.at[it + 1, p, rows], dst_ref=own.at[it + 1, p, rows],
+            src_ref=there, dst_ref=there,
             send_sem=sent.at[1], recv_sem=recv.at[group, ROWS + min(o, 1)],
             device_id=device(dz=dz, dh=dh), device_id_type=MESH,
         )
@@ -294,7 +297,11 @@
         total = acc[p, rows]
         for o in range(7):
             total = total + parts_in[group, o].astype(F32)
-        own[it + 1, p, rows] = ((ints[p].astype(F32) + total) / den[p]).astype(BF16)
+        fresh = ((ints[p].astype(F32) + total) / den[p]).astype(BF16)
+        if it == ITERS - 1:
+            out_ref[0, p, rows] = fresh
+        else:
+            own[it + 1, p, rows] = fresh
         for o in range(7):
             ag_copy(group, o).start()
 
@@ -349,8 +356,7 @@
                     events[name](which)
                 return
             middle = (low + high) // 2
-            pl.when(number < middle)(lambda: happen(low, middle))
-            pl.when(number >= middle)(lambda: happen(middle, high))
+            lax.cond(number < middle, lambda: happen(low, middle), lambda: happen(middle, high))
 
         happen(0, 8 * GROUPS)
 
@@ -373,43 +379,35 @@
 
     share_own(0)
     begin(0)
+    first_load(1).wait()
     share_own(1)
     lax.fori_loop(0, 8 * GROUPS, turn, 0)
     scatter(GROUPS - 1)
     take_rows_first(GROUPS - 2)
     take_rows_rest(GROUPS - 2)
-    writes = [
-        pltpu.make_async_copy(own.at[ITERS, p], out_hbm.at[0, p], edge.at[4 + p])
-        for p in range(PAIRS)
-    ]
-    writes[0].start()
     update(GROUPS - 1)
     take_rows_first(GROUPS - 1)
     take_rows_rest(GROUPS - 1)
-    writes[1].start()
 
     there = cur.at[:, pl.ds(0, 15)]
     pltpu.make_async_copy(there, there, sent.at[0]).wait()
     for back in (parts_out, parts_in):
         pltpu.make_async_copy(back, back, sent.at[1]).wait()
-    for one in writes:
-        one.wait()
 
 
 def on_device(*args):
     anywhere = pl.BlockSpec(memory_space=pl.ANY)
-    smem = pl.BlockSpec(memory_space=pltpu.SMEM)
     dma = pltpu.SemaphoreType.DMA
     return pl.pallas_call(
         kernel,
-        out_shape=jax.ShapeDtypeStruct((1, PAIRS, NV, NV), BF16),
-        in_specs=[anywhere] * 4 + [smem, anywhere, anywhere],
-        out_specs=anywhere,
+        out_shape=pltpu.VMEM((1, PAIRS, NV, NV), BF16),
+        in_specs=[anywhere] * 7,
+        out_specs=pl.BlockSpec(memory_space=pltpu.VMEM),
         scratch_shapes=[
             pltpu.VMEM((ITERS, NK, PAIRS, NV, NV), BF16),
             pltpu.VMEM((NK, LOCAL_AUX, NV, NV), BF16),
             pltpu.VMEM((NK, LOCAL_AUX, NV, NV), BF16),
-            pltpu.VMEM((ITERS + 1, PAIRS, NV, NV), BF16),
+            pltpu.VMEM((ITERS, PAIRS, NV, NV), BF16),
             pltpu.VMEM((2 * LOCAL_AUX * NV, NV), BF16),
             pltpu.VMEM((PAIRS, NV, NV), F32),
             pltpu.VMEM((GROUPS, 7, CHUNK, NV), BF16),
@@ -418,10 +416,11 @@
             pltpu.VMEM((PAIRS, CHUNK, NV), F32),
             pltpu.VMEM((NK, NV), F32),
             pltpu.SMEM((8, NK), jnp.int32),
+            pltpu.SMEM((PAIRS,), F32),
             dma((2,)),
             dma((GROUPS, ARRIVALS)),
             dma((8, 2)),
-            dma((6,)),
+            dma((7,)),
         ],
         compiler_params=pltpu.CompilerParams(
             collective_id=0, has_side_effects=True, vmem_limit_bytes=60 * 2**20

time: 94.2 us -> 90.8 us (0.964)
  Pallas kernels: 92.1 us -> 89.8 us
  local copies, waits for them, and re-layouts: 1.94 us -> 0.82 us
    pallas_call x1, Pallas kernels: 92.1 us -> 89.8 us  [on_device(): pl.pallas_call(kernel, out_shape=pltpu.VMEM((1, PAIRS, NV, NV), BF16), in...]
    unnamed x1, local copies, waits for them, and re-layouts: 1.94 us -> 0.82 us
where the time goes in v3:
time: 90.8 us; the launch traced here: 90.7 us
  Pallas kernels  89.8 us (99%)
    pallas_call x1, Pallas kernels, on_device(): pl.pallas_call(kernel, out_shape=pltpu.VMEM((1, PAIRS, NV, NV), BF16), in...  89.8 us

profile of v3, /device:TPU:0, one launch (start us, length us, event | category | flops | bytes accessed | tf_op | source)
XLA Modules:
  0.0 90.7 jit_solution(11411350670596478978)
XLA Ops:
  0.0 89.8 %ladder.1 = bf16[1,2,384,384]{3,2,1,0:T(8,128)(2,1)S(1)} custom-call(bf16[1,2,384,384]{3,2,1,0:T(8,128)(2,1)} %amp_hbm.1, bf16[1,2,384,384]{3,2,1,0:T(8,128)(2,1)} %int_hbm.1, bf16[1,16,2,384,384]{4,3,2,1,0:T(8,128)(2,1)} %left_hbm.1, bf16[1,16,2,384,384]{4,3,2,1,0:T(8,128)(2,1)} %right_hbm.1, f32[2]{0:T(128)} %pair_hbm.1, f32[16,384]{1,0:T(8,128)} %virt_hbm.1, ...), custom_call_target="tpu_custom_call" | custom-call | flops 30000001024 | bytes 40000000 | tf_op jit(solution)/shard_map/ladder/pallas_call | solution.py:401
  89.8 0.8 copy.9
